TPU v7x, 256 devices: a whole 4x4x8 slice. The times are simulated.
256 devices in a mesh: species: 8 (over z), wave: 32 (over y, x, core).
Axes of the slice: x: 4, y: 4, z: 8, core: 2. Of those that a mesh axis runs over, the one named last changes fastest.
Arguments:
- dest_tiles: int32 [8, 1024, 1], P('species', 'wave'), may hold values from 0 to 31; in each aligned block of 32 rows (0 to 31, 32 to 63, ..., all dimensions but the last counted through in order) at most 2 rows name the same one
- line_counts: int32 [8, 1024], P('species', 'wave'), may hold values from 32 to 128
- wing_widths: int32 [8, 1024], P('species', 'wave'), may hold values from 16 to 64
- species_ids: int32 [8, 131072], P('species', 'wave'), may hold values from 0 to 3
- offsets: float32 [8, 131072], P('species', 'wave'), may hold values from 0 to 256
- strengths: float32 [8, 131072], P('species', 'wave'), may hold values from 0.01 to 0.2
- doppler: float32 [8, 131072], P('species', 'wave'), may hold values from 0.5 to 6
- lorentz: float32 [8, 131072], P('species', 'wave'), may hold values from 0.1 to 4
- energy: float32 [8, 131072], P('species', 'wave'), may hold values from 0.05 to 3
- temp_scale: float32 [16], replicated, may hold values from 0.5 to 2
- press_scale: float32 [16], replicated, may hold values from 0.2 to 4
- inverse_temp: float32 [16], replicated, may hold values from 0.2 to 1.5
- abundances: float32 [4, 8, 4, 16], P(None, 'species'), may hold values from 0.05 to 1
Outputs:
- opacity: float32 [4, 16, 8192], P(None, 'species', 'wave')
Inputs may be any that keep to these rules, and one draw needn't show every extreme that they name: `dest_tiles`: within one device's 32 blocks no tile is named more than 2 times.
All inputs are finite; a program needn't handle non-finite values.
Results may differ from a plain program's by a relative error of at most 0.0004.
Values sent between devices are 32-bit elements; how exact they have to be, the bound alone decides.
No kernel may reach another device: no remote copies, remote signals or barrier semaphores. Data moves between devices by JAX's collectives and lax.ppermute only.
A program may use at most 64 MiB of HBM per device.

v0:
```python
import jax
import jax.numpy as jnp
from jax import lax
from jax.experimental import pallas as pl
from jax.experimental.pallas import tpu as pltpu
from jax.sharding import PartitionSpec as P

TILE = 256
TP = 16
MIXES = 4
SUB = 4
HALO = 64
LANES = 128
FIELDS = 8
BUCKET = 16
NBUCKET = TILE // BUCKET
ROWS = 2 * HALO + BUCKET
COLS = 2 * NBUCKET * MIXES
STEP = 8
CLASSES = HALO // STEP
UNROLL = 16
GROUP = 4
PREP = 2
POUR = 4

VMEM = pl.BlockSpec(memory_space=pltpu.VMEM)
SMEM = pl.BlockSpec(memory_space=pltpu.SMEM)


def tables_kernel(abundance, temp, press, invtemp, tables):
    at = lax.broadcasted_iota(jnp.int32, (TP, LANES), 0)
    for which, values in enumerate((temp, press, invtemp)):
        made = jnp.zeros((TP, LANES), jnp.float32)
        for t in range(TP):
            made = jnp.where(at == t, values[t], made)
        tables[TP * SUB + 2 * which] = made[:FIELDS]
        tables[TP * SUB + 2 * which + 1] = made[FIELDS:]
    mix = lax.bitwise_and(lax.broadcasted_iota(jnp.int32, (FIELDS, LANES), 0), MIXES - 1)

    def spread(t, _):
        for s in range(SUB):
            made = jnp.zeros((FIELDS, LANES), jnp.float32)
            for m in range(MIXES):
                made = jnp.where(mix == m, abundance[m, 0, s, t], made)
            tables[t * SUB + s] = made
        return 0

    lax.fori_loop(0, TP, spread, 0, unroll=4)


def pack_kernel(nblocks, dest, counts, reach, off, dop, lor, ene, stre, spec, out, used):
    ntiles = used.shape[0]
    empty = jnp.zeros((FIELDS, LANES), jnp.float32)

    def clear(tile, _):
        used[tile] = 0
        out[2 * tile] = empty
        out[2 * tile + 1] = empty
        return 0

    lax.fori_loop(0, ntiles, clear, 0, unroll=4)

    def place(block, _):
        tile = dest[block]
        rank = used[tile]
        used[tile] = rank + 1
        slot = 2 * tile + rank
        at = pl.ds(block, 1)
        out[slot, 0:1, :] = off[at, :]
        out[slot, 1:2, :] = dop[at, :]
        out[slot, 2:3, :] = lor[at, :]
        out[slot, 3:4, :] = ene[at, :]
        out[slot, 4:5, :] = stre[at, :]
        out[slot, 5:6, :] = spec[at, :].astype(jnp.float32)
        out[slot, 6:7, :] = jnp.full((1, LANES), reach[block].astype(jnp.float32))
        out[slot, 7:8, :] = jnp.full((1, LANES), counts[block].astype(jnp.float32))
        return 0

    lax.fori_loop(0, nblocks, place, 0, unroll=4)


def opacity_kernel(nslots, scalars, recs, tables, acc, order, first, lines, live, prm, hot, sq):
    def klass(i):
        wing = scalars[0, i]
        c = jnp.minimum(lax.shift_right_logical(wing, 3) + 1, CLASSES)
        return jnp.where(wing > 0, c, 0)

    def count(i, _):
        c = klass(i)
        first[c] = first[c] + 1
        lines[c] = lines[c] + scalars[1, i]
        return 0

    for c in range(CLASSES + 1):
        first[c] = 0
        lines[c] = 0
    lax.fori_loop(0, nslots, count, 0, unroll=8)
    slots, total = jnp.int32(0), jnp.int32(0)
    ends = {CLASSES + 1: total}
    for c in range(CLASSES, 0, -1):
        held = first[c]
        first[c] = slots
        slots = slots + held
        total = total + lines[c]
        ends[c] = lax.div(total + (GROUP * LANES - 1), GROUP * LANES)
    first[0] = slots

    def place(i, _):
        c = klass(i)
        at = first[c]
        order[at] = i
        first[c] = at + 1
        return 0

    lax.fori_loop(0, nslots, place, 0, unroll=8)

    row = lax.broadcasted_iota(jnp.int32, (FIELDS, LANES), 0)
    lane = lax.broadcasted_iota(jnp.int32, (FIELDS, LANES), 1)
    blank = jnp.where((row == 1) | (row == 2), 1.0, 0.0)

    def empty(i, _):
        live[i] = blank
        return 0

    lax.fori_loop(0, live.shape[0], empty, 0, unroll=6)

    def pour(i, filled):
        for j in range(POUR):
            slot = order[POUR * i + j]
            held = scalars[1, slot]
            into = lax.shift_right_logical(filled, 7)
            turn = lax.bitwise_and(filled, LANES - 1)
            side = lax.bitwise_and(lax.shift_right_logical(slot, 1), 1)
            record = jnp.where(row == 7, side.astype(jnp.float32), recs[slot])
            turned = pltpu.roll(record, turn, 1)
            pltpu.store(live.at[into], turned, mask=(lane >= turn) & (lane < turn + held))
            pltpu.store(live.at[into + 1], turned, mask=lane < turn + held - LANES)
            filled = filled + held
        return filled

    lax.fori_loop(0, lax.div(slots + (POUR - 1), POUR), pour, jnp.int32(0))

    def wipe(t, _):
        acc[t] = jnp.zeros(acc.shape[1:], jnp.float32)
        return 0

    lax.fori_loop(0, TP, wipe, 0)

    def column(which):
        made = jnp.concatenate([tables[TP * SUB + 2 * which], tables[TP * SUB + 2 * which + 1]], axis=0)
        return jnp.concatenate([made] * GROUP, axis=1)

    tscale, pscale, invt = column(0), column(1), column(2)
    bucket_row = lax.shift_right_logical(lax.broadcasted_iota(jnp.int32, (COLS, GROUP * LANES), 0), 2)
    bucket_row = bucket_row.astype(jnp.float32)

    def prepare(p):
        rec = jnp.concatenate([live[GROUP * p + j] for j in range(GROUP)], axis=1)
        dop, lor, energy = rec[1:2], rec[2:3], rec[3:4]
        gauss = 2.35482 * (tscale * dop)
        lorz = 2.0 * (pscale * lor)
        g2, l2 = gauss * gauss, lorz * lorz
        g4, l4 = g2 * g2, l2 * l2
        fifth = (
            g4 * gauss
            + 2.69269 * g4 * lorz
            + 2.42843 * (g2 * gauss) * l2
            + 4.47163 * g2 * (l2 * lorz)
            + 0.07842 * gauss * l4
            + l4 * lorz
        )
        width = jnp.exp(0.2 * jnp.log(fifth))
        inv = 1.0 / width
        q = lorz * inv
        mixing = q * (1.36603 + q * (-0.47719 + q * 0.11116))
        prm[p, 0] = mixing * (0.15915494 * width)
        prm[p, 1] = 0.25 * (width * width)
        prm[p, 2] = (1.0 - mixing) * (0.9394373 * inv)
        prm[p, 3] = (-2.7725887 * 1.4426950408889634) * (inv * inv)
        prm[p, 4] = jnp.exp(-(invt * energy))

    def prepare_some(i, _):
        for j in range(PREP):
            prepare(PREP * i + j)
        return 0

    lax.fori_loop(0, lax.div(ends[1] + (PREP - 1), PREP), prepare_some, 0)

    def group(p, far):
        n = 2 * far + BUCKET
        rec = jnp.concatenate([live[GROUP * p + j] for j in range(GROUP)], axis=1)
        center, strength, kind, limit, side = rec[0:1], rec[4:5], rec[5:6], rec[6:7], rec[7:8]
        bucket = jnp.minimum(jnp.floor(center * (1.0 / BUCKET)), NBUCKET - 1.0)
        frac = center - BUCKET * bucket
        hot[...] = jnp.where(bucket_row == bucket + NBUCKET * side, 1.0, 0.0).astype(jnp.bfloat16)
        point = lax.broadcasted_iota(jnp.int32, (n, GROUP * LANES), 0).astype(jnp.float32) - float(far)
        x = point - frac
        sq[0:n] = jnp.where(jnp.abs(x) <= limit, x * x, jnp.inf)

        def at_point(t, _):
            at = pl.ds(t, 1)
            picked = jnp.zeros((8, GROUP * LANES), jnp.float32)
            for s in range(SUB):
                ab = tables[t * SUB + s]
                picked = jnp.where(kind == float(s), jnp.concatenate([ab] * GROUP, axis=1), picked)
            w8 = picked * strength * prm[p, 4, at, :]
            w16 = jnp.concatenate([w8, w8], axis=0).astype(jnp.bfloat16)
            wide = hot[...] * jnp.concatenate([w16] * (COLS // 16), axis=0)
            a, b, g, h = [prm[p, j, at, :] for j in range(4)]
            s2 = sq[0:n]
            shape = a * pl.reciprocal(s2 + b, approx=True) + g * jnp.exp2(s2 * h)
            part = lax.dot_general(
                shape.astype(jnp.bfloat16),
                wide,
                (((1,), (1,)), ((), ())),
                preferred_element_type=jnp.float32,
            )
            low = HALO - far
            acc[t, low : low + n, 0:COLS] = acc[t, low : low + n, 0:COLS] + part
            return 0

        lax.fori_loop(0, TP, at_point, 0, unroll=UNROLL)

    for c in range(CLASSES, 0, -1):
        def body(p, _, far=STEP * c):
            group(p, far)
            return 0

        lax.fori_loop(ends[c + 1], ends[c], body, 0)


def fold_kernel(core, acc, own, other):
    lane = lax.broadcasted_iota(jnp.int32, (BUCKET, LANES), 1)
    body, wing = NBUCKET * MIXES, (HALO // BUCKET) * MIXES
    half = body + wing
    for t in range(TP):
        low = acc[t, 0:BUCKET, :]
        high = jnp.zeros((BUCKET, LANES), jnp.float32)
        for i in range(1, ROWS // BUCKET):
            turned = pltpu.roll(acc[t, BUCKET * i : BUCKET * (i + 1), :], MIXES * i, 1)
            passed = lane < MIXES * i
            low = low + jnp.where(passed, 0.0, turned)
            high = high + jnp.where(passed, turned, 0.0)
        second = jnp.where(lane < LANES - half, pltpu.roll(low, LANES - half, 1), pltpu.roll(high, LANES - half, 1))
        first = jnp.where((lane < body) | (lane >= LANES - wing), pltpu.roll(low, LANES - wing, 1), 0.0)
        own[t] = jnp.where(core == 0, first, second)
        other[t] = jnp.where(core == 0, second, first)


def core_number():
    return lax.rem(lax.axis_index("wave"), 2)


def opacity(scalars, recs, tables):
    nslots = recs.shape[0]
    groups = PREP * (-(-nslots // (GROUP * PREP)))

    def kernel(scalars, recs, tables, own, other, acc, *scratch):
        opacity_kernel(nslots, scalars, recs, tables, acc, *scratch)
        fold_kernel(core_number(), acc, own, other)

    return pl.pallas_call(
        kernel,
        out_shape=[jax.ShapeDtypeStruct((TP, BUCKET, LANES), jnp.float32)] * 2,
        in_specs=[SMEM, VMEM, VMEM],
        out_specs=[VMEM, VMEM],
        scratch_shapes=[
            pltpu.VMEM((TP, ROWS, LANES), jnp.float32),
            pltpu.SMEM((nslots,), jnp.int32),
            pltpu.SMEM((CLASSES + 1,), jnp.int32),
            pltpu.SMEM((CLASSES + 1,), jnp.int32),
            pltpu.VMEM((GROUP * groups + 2, FIELDS, LANES), jnp.float32),
            pltpu.VMEM((groups, 5, TP, GROUP * LANES), jnp.float32),
            pltpu.VMEM((COLS, GROUP * LANES), jnp.bfloat16),
            pltpu.VMEM((ROWS, GROUP * LANES), jnp.float32),
        ],
        compiler_params=pltpu.CompilerParams(vmem_limit_bytes=24 * 2**20),
        name="opacity",
    )(scalars, recs, tables)


def per_device(
    dest_tiles,
    line_counts,
    wing_widths,
    species_ids,
    offsets,
    strengths,
    doppler,
    lorentz,
    energy,
    temp_scale,
    press_scale,
    inverse_temp,
    abundances,
):
    ntiles = lax.axis_size("wave")
    nblocks = dest_tiles.shape[1]

    def rows(array):
        return array.reshape(nblocks, LANES)

    def kernel(*refs):
        tables_kernel(*refs[9:13], refs[14])
        pack_kernel(nblocks, *refs[:9], refs[13], refs[15])

    packed, tables = pl.pallas_call(
        kernel,
        out_shape=[
            jax.ShapeDtypeStruct((2 * ntiles, FIELDS, LANES), jnp.float32),
            jax.ShapeDtypeStruct((TP * SUB + 6, FIELDS, LANES), jnp.float32),
        ],
        in_specs=[SMEM] * 3 + [VMEM] * 6 + [SMEM] * 4,
        out_specs=[VMEM] * 2,
        scratch_shapes=[pltpu.SMEM((ntiles,), jnp.int32)],
        name="pack",
    )(
        dest_tiles.reshape(nblocks),
        line_counts.reshape(nblocks),
        wing_widths.reshape(nblocks),
        rows(offsets),
        rows(doppler),
        rows(lorentz),
        rows(energy),
        rows(strengths),
        rows(species_ids),
        abundances,
        temp_scale,
        press_scale,
        inverse_temp,
    )
    cores = [list(range(core, ntiles, 2)) for core in range(2)]
    recs = lax.all_to_all(packed, "wave", split_axis=0, concat_axis=0, tiled=True, axis_index_groups=cores)
    scalars = jnp.transpose(recs[:, 6:8, 0]).astype(jnp.int32)
    own, other = opacity(scalars, recs, tables)
    twin = lax.ppermute(other, "wave", [(i, i ^ 1) for i in range(ntiles)])
    shares = lax.all_to_all(own + twin, "species", split_axis=0, concat_axis=0, tiled=True)
    mine = jnp.sum(shares.reshape(-1, TP // lax.axis_size("species"), BUCKET, LANES), axis=0)

    body = NBUCKET * MIXES
    across = [(i, i + 1) for i in range(1, ntiles - 1, 2)]
    across = across + [(i + 1, i) for i in range(1, ntiles - 1, 2)]
    middle = mine[:, :, :body] + lax.ppermute(mine[:, :, body:], "wave", across)
    middle = middle.reshape(-1, BUCKET, NBUCKET, MIXES)
    return jnp.transpose(middle, (3, 0, 2, 1)).reshape(MIXES, -1, TILE)


def solution(mesh):
    line = P("species", "wave")
    return jax.shard_map(
        per_device,
        mesh=mesh,
        in_specs=(P("species", "wave", None),) + (line,) * 8 + (P(), P(), P(), P(None, "species", None, None)),
        out_specs=P(None, "species", "wave"),
        check_vma=False,
    )
```

profile of v0, /device:TPU:16, one launch (start us, length us, event | category | flops | bytes accessed | tf_op | source)
XLA Modules:
  0.0 57.8 jit_solution(16113503435449749346)
XLA Ops:
  0.0 2.3 %pack.1 = (f32[64,8,128]{2,1,0:T(8,128)}, f32[70,8,128]{2,1,0:T(8,128)}) custom-call(s32[32]{0:T(128)} %bitcast.27, s32[32]{0:T(128)} %bitcast.28, s32[32]{0:T(128)} %bitcast.29, f32[32,128]{1,0:T(8,128)} %bitcast.21, f32[32,128]{1,0:T(8,128)} %bitcast.22, f32[32,128]{1,0:T(8,128)} %bitcast.23, f32[32,128]{1,0:T(8,128)} %bitcast.24, f32[32,128]{1,0:T(8,128)} %bitcast.25, ...), custom_call_target="tpu_custom_call" | custom-call | tf_op jit(solution)/shard_map/pack/pallas_call | solution.py:307
  2.3 0.0 copy-start
  2.3 13.7 %all_to_all.10.recs = f32[64,8,128]{2,1,0:T(8,128)S(1)} all-to-all(f32[64,8,128]{2,1,0:T(8,128)} %get-tuple-element.9), channel_id=1, replica_groups={{0,2,4,6,8,10,12,14,16,18,20,22,24,26,28,30},{1,3,5,7,9,11,13,15,17,19,..., dimensions={0} | all-to-all | bytes 524288 | tf_op jit(solution)/shard_map/all_to_all | solution.py:333
  16.0 0.1 copy.21
  16.1 0.0 copy-done
  16.1 15.2 %opacity.1 = (f32[16,16,128]{2,1,0:T(8,128)S(1)}, f32[16,16,128]{2,1,0:T(8,128)S(1)}) custom-call(s32[2,64]{1,0:T(2,128)S(1)} %bitcast.18, f32[64,8,128]{2,1,0:T(8,128)S(1)} %all_to_all.10.recs, f32[70,8,128]{2,1,0:T(8,128)S(1)} %copy-done), custom_call_target="tpu_custom_call" | custom-call | tf_op jit(solution)/shard_map/opacity/pallas_call | solution.py:262
  31.3 0.1 collective-permute-start
  31.4 1.3 %collective-permute-done = f32[16,16,128]{2,1,0:T(8,128)S(1)} collective-permute-done((f32[16,16,128]{2,1,0:T(8,128)S(1)}, f32[16,16,128]{2,1,0:T(8,128)S(1)}, u32[]{:S(2)}, u32[]{:S(2)}) %collective-permute-start) | collective-permute-done | bytes 131104 | tf_op jit(solution)/shard_map/ppermute | solution.py:336
  32.7 17.0 %all_to_all.11 = f32[16,16,128]{2,1,0:T(8,128)S(1)} all-to-all(f32[16,16,128]{2,1,0:T(8,128)S(1)} %add.6), channel_id=1, replica_groups=mesh['species'=8,'wave'=32] {'species'}, dimensions={0} | all-to-all | bytes 262144 | tf_op jit(solution)/shard_map/all_to_all | solution.py:337
  49.7 0.1 slice.14
  49.8 1.9 %collective-permute-start.1 = (f32[2,16,64]{2,1,0:T(8,128)S(1)}, f32[2,16,64]{2,1,0:T(8,128)S(1)}, u32[]{:S(2)}, u32[]{:S(2)}) collective-permute-start(f32[2,16,64]{2,1,0:T(8,128)S(1)} %slice.14), channel_id=1, source_target_pairs={{1,2},{3,4},{5,6},{7,8},{9,10},{11,12},{13,14},{15,16},{17,18},{19... | collective-permute-start | bytes 24584 | tf_op jit(solution)/shard_map/ppermute | solution.py:343
  51.7 5.2 %collective-permute-done.1 = f32[2,16,64]{2,1,0:T(8,128)S(1)} collective-permute-done((f32[2,16,64]{2,1,0:T(8,128)S(1)}, f32[2,16,64]{2,1,0:T(8,128)S(1)}, u32[]{:S(2)}, u32[]{:S(2)}) %collective-permute-start.1) | collective-permute-done | bytes 8224 | tf_op jit(solution)/shard_map/ppermute | solution.py:343
  57.0 0.1 copy.22
  57.1 0.7 %reshape.48 = f32[4,2,256]{2,1,0:T(2,128)} reshape(f32[4,2,16,16]{3,2,1,0:T(8,128)S(1)} %copy.23) | data formatting | bytes 16384 | tf_op jit(solution)/shard_map/reshape | solution.py:345
  (5 shorter events, 0.1 us)
Async XLA Ops:
  2.3 13.8 %copy-start = (f32[70,8,128]{2,1,0:T(8,128)S(1)}, f32[70,8,128]{2,1,0:T(8,128)}, u32[]{:S(2)}) copy-start(f32[70,8,128]{2,1,0:T(8,128)} %get-tuple-element.10.tables) | copy-start | bytes 860164
  31.3 1.4 %collective-permute-start = (f32[16,16,128]{2,1,0:T(8,128)S(1)}, f32[16,16,128]{2,1,0:T(8,128)S(1)}, u32[]{:S(2)}, u32[]{:S(2)}) collective-permute-start(f32[16,16,128]{2,1,0:T(8,128)S(1)} %get-tuple-element.12), channel_id=1, source_target_pairs={{0,1},{1,0},{2,3},{3,2},{4,5},{5,4},{6,7},{7,6},{8,9},{9,8},{10,11... | collective-permute-start | bytes 393224 | tf_op jit(solution)/shard_map/ppermute | solution.py:336
  49.8 7.2 %collective-permute-start.1 = (f32[2,16,64]{2,1,0:T(8,128)S(1)}, f32[2,16,64]{2,1,0:T(8,128)S(1)}, u32[]{:S(2)}, u32[]{:S(2)}) collective-permute-start(f32[2,16,64]{2,1,0:T(8,128)S(1)} %slice.14), channel_id=1, source_target_pairs={{1,2},{3,4},{5,6},{7,8},{9,10},{11,12},{13,14},{15,16},{17,18},{19... | collective-permute-start | bytes 24584 | tf_op jit(solution)/shard_map/ppermute | solution.py:343
where the time goes:
time: 58.9 us; the launch traced here: 57.8 us
  blocking collectives  30.7 us (52%)
  Pallas kernels  17.4 us (30%)
  waiting for transfers between devices  6.57 us (11%)
  starting transfers between devices  2 us (3%)
  local copies, waits for them, and re-layouts  0.96 us (2%)
    all_to_all x1, blocking collectives, per_device(): lax.all_to_all(own + twin, 'species', split_axis=0, concat_axis=0, tiled=...  17 us
    pallas_call x1, Pallas kernels, opacity(): pl.pallas_call(kernel, out_shape=[jax.ShapeDtypeStruct((TP, BUCKET, LANES...  15.2 us
    all_to_all x1, blocking collectives, per_device(): lax.all_to_all(packed, 'wave', split_axis=0, concat_axis=0, tiled=True, a...  13.7 us
    ppermute x1, waiting for transfers between devices, per_device(): middle = mine[:, :, :body] + lax.ppermute(mine[:, :, body:], 'wave', across)  5.24 us
    pallas_call x1, Pallas kernels, per_device(): pl.pallas_call(kernel, out_shape=[jax.ShapeDtypeStruct((2 * ntiles, FIELD...  2.29 us
    ppermute x1, starting transfers between devices, per_device(): middle = mine[:, :, :body] + lax.ppermute(mine[:, :, body:], 'wave', across)  1.91 us
    ppermute x1, waiting for transfers between devices, per_device(): twin = lax.ppermute(other, 'wave', [(i, i ^ 1) for i in range(ntiles)])  1.33 us
  transfers between devices with their start and end apart: 2, of which 2 were waited for; matrix products, arithmetic and copies ran while one was open for 0% of the time, Pallas kernels for 0%

commit v1 on v0

--- a/solution.py
+++ b/solution.py
@@ -21,7 +21,7 @@
 UNROLL = 16
 GROUP = 4
 PREP = 2
-POUR = 4
+POUR = 8
 
 VMEM = pl.BlockSpec(memory_space=pltpu.VMEM)
 SMEM = pl.BlockSpec(memory_space=pltpu.SMEM)
@@ -45,7 +45,7 @@
             tables[t * SUB + s] = made
         return 0
 
-    lax.fori_loop(0, TP, spread, 0, unroll=4)
+    lax.fori_loop(0, TP, spread, 0, unroll=16)
 
 
 def pack_kernel(nblocks, dest, counts, reach, off, dop, lor, ene, stre, spec, out, used):
@@ -229,10 +229,13 @@
         lax.fori_loop(ends[c + 1], ends[c], body, 0)
 
 
-def fold_kernel(core, acc, own, other):
+def fold_kernel(core, inner, acc, own, other, takes):
     lane = lax.broadcasted_iota(jnp.int32, (BUCKET, LANES), 1)
     body, wing = NBUCKET * MIXES, (HALO // BUCKET) * MIXES
     half = body + wing
+    begin = core * (body - wing)
+    at = lax.broadcasted_iota(jnp.int32, takes.shape, 1)
+    takes[...] = jnp.where((at >= begin) & (at < begin + wing * inner), 1.0, 0.0)
     for t in range(TP):
         low = acc[t, 0:BUCKET, :]
         high = jnp.zeros((BUCKET, LANES), jnp.float32)
@@ -248,22 +251,25 @@
 
 
 def core_number():
-    return lax.rem(lax.axis_index("wave"), 2)
+    me, count = lax.axis_index("wave"), lax.axis_size("wave")
+    inner = jnp.where((me > 0) & (me < count - 1), 1, 0)
+    return lax.rem(me, 2), inner
 
 
 def opacity(scalars, recs, tables):
     nslots = recs.shape[0]
     groups = PREP * (-(-nslots // (GROUP * PREP)))
 
-    def kernel(scalars, recs, tables, own, other, acc, *scratch):
+    def kernel(scalars, recs, tables, own, other, takes, acc, *scratch):
         opacity_kernel(nslots, scalars, recs, tables, acc, *scratch)
-        fold_kernel(core_number(), acc, own, other)
+        fold_kernel(*core_number(), acc, own, other, takes)
 
     return pl.pallas_call(
         kernel,
-        out_shape=[jax.ShapeDtypeStruct((TP, BUCKET, LANES), jnp.float32)] * 2,
+        out_shape=[jax.ShapeDtypeStruct((TP, BUCKET, LANES), jnp.float32)] * 2
+        + [jax.ShapeDtypeStruct((BUCKET, NBUCKET * MIXES), jnp.float32)],
         in_specs=[SMEM, VMEM, VMEM],
-        out_specs=[VMEM, VMEM],
+        out_specs=[VMEM] * 3,
         scratch_shapes=[
             pltpu.VMEM((TP, ROWS, LANES), jnp.float32),
             pltpu.SMEM((nslots,), jnp.int32),
@@ -332,15 +338,15 @@
     cores = [list(range(core, ntiles, 2)) for core in range(2)]
     recs = lax.all_to_all(packed, "wave", split_axis=0, concat_axis=0, tiled=True, axis_index_groups=cores)
     scalars = jnp.transpose(recs[:, 6:8, 0]).astype(jnp.int32)
-    own, other = opacity(scalars, recs, tables)
+    own, other, takes = opacity(scalars, recs, tables)
     twin = lax.ppermute(other, "wave", [(i, i ^ 1) for i in range(ntiles)])
     shares = lax.all_to_all(own + twin, "species", split_axis=0, concat_axis=0, tiled=True)
     mine = jnp.sum(shares.reshape(-1, TP // lax.axis_size("species"), BUCKET, LANES), axis=0)
 
     body = NBUCKET * MIXES
-    across = [(i, i + 1) for i in range(1, ntiles - 1, 2)]
-    across = across + [(i + 1, i) for i in range(1, ntiles - 1, 2)]
-    middle = mine[:, :, :body] + lax.ppermute(mine[:, :, body:], "wave", across)
+    pairs = [[i, i + 1] for i in range(1, ntiles - 1, 2)] + [[0, ntiles - 1]]
+    wings = lax.all_gather(mine[:, :, body:], "wave", axis_index_groups=pairs)
+    middle = mine[:, :, :body] + (wings[0] + wings[1]) * takes
     middle = middle.reshape(-1, BUCKET, NBUCKET, MIXES)
     return jnp.transpose(middle, (3, 0, 2, 1)).reshape(MIXES, -1, TILE)
 

time: 58.9 us -> 57.1 us (0.969)
  the two profiles are of different devices: /device:TPU:16 before, /device:TPU:8 now
where the time goes in v1:
time: 57.1 us; the launch traced here: 57.3 us
  blocking collectives  38.4 us (67%)
  Pallas kernels  16.4 us (29%)
  waiting for transfers between devices  1.33 us (2%)
  local copies, waits for them, and re-layouts  0.96 us (2%)
    all_to_all x1, blocking collectives, per_device(): lax.all_to_all(own + twin, 'species', split_axis=0, concat_axis=0, tiled=...  17.9 us
    all_to_all x1, blocking collectives, per_device(): lax.all_to_all(packed, 'wave', split_axis=0, concat_axis=0, tiled=True, a...  14.5 us
    pallas_call x1, Pallas kernels, opacity(): pl.pallas_call(kernel, out_shape=[jax.ShapeDtypeStruct((TP, BUCKET, LANES...  14.3 us
    all_gather x1, blocking collectives, per_device(): wings = lax.all_gather(mine[:, :, body:], 'wave', axis_index_groups=pairs)  5.94 us
    pallas_call x1, Pallas kernels, per_device(): pl.pallas_call(kernel, out_shape=[jax.ShapeDtypeStruct((2 * ntiles, FIELD...  2.11 us
    ppermute x1, waiting for transfers between devices, per_device(): twin = lax.ppermute(other, 'wave', [(i, i ^ 1) for i in range(ntiles)])  1.33 us
  transfers between devices with their start and end apart: 1, of which 1 were waited for; matrix products, arithmetic and copies ran while one was open for 0% of the time, Pallas kernels for 0%

profile of v1, /device:TPU:8, one launch (start us, length us, event | category | flops | bytes accessed | tf_op | source)
XLA Modules:
  0.0 57.3 jit_solution(16092865383970953488)
XLA Ops:
  0.0 2.1 %pack.1 = (f32[64,8,128]{2,1,0:T(8,128)}, f32[70,8,128]{2,1,0:T(8,128)}) custom-call(s32[32]{0:T(128)} %bitcast.27, s32[32]{0:T(128)} %bitcast.28, s32[32]{0:T(128)} %bitcast.29, f32[32,128]{1,0:T(8,128)} %bitcast.21, f32[32,128]{1,0:T(8,128)} %bitcast.22, f32[32,128]{1,0:T(8,128)} %bitcast.23, f32[32,128]{1,0:T(8,128)} %bitcast.24, f32[32,128]{1,0:T(8,128)} %bitcast.25, ...), custom_call_target="tpu_custom_call" | custom-call | tf_op jit(solution)/shard_map/pack/pallas_call | solution.py:313
  2.1 0.0 copy-start
  2.1 14.5 %all_to_all.10.recs = f32[64,8,128]{2,1,0:T(8,128)S(1)} all-to-all(f32[64,8,128]{2,1,0:T(8,128)} %get-tuple-element.10), channel_id=1, replica_groups={{0,2,4,6,8,10,12,14,16,18,20,22,24,26,28,30},{1,3,5,7,9,11,13,15,17,19,..., dimensions={0} | all-to-all | bytes 524288 | tf_op jit(solution)/shard_map/all_to_all | solution.py:339
  16.7 0.1 copy.23
  16.7 0.0 copy-done
  16.7 14.3 %opacity.1 = (f32[16,16,128]{2,1,0:T(8,128)S(1)}, f32[16,16,128]{2,1,0:T(8,128)S(1)}, f32[16,64]{1,0:T(8,128)S(1)}) custom-call(s32[2,64]{1,0:T(2,128)S(1)} %bitcast.18, f32[64,8,128]{2,1,0:T(8,128)S(1)} %all_to_all.10.recs, f32[70,8,128]{2,1,0:T(8,128)S(1)} %copy-done), custom_call_target="tpu_custom_call" | custom-call | tf_op jit(solution)/shard_map/opacity/pallas_call | solution.py:267
  31.1 0.1 collective-permute-start
  31.2 1.3 %collective-permute-done = f32[16,16,128]{2,1,0:T(8,128)S(1)} collective-permute-done((f32[16,16,128]{2,1,0:T(8,128)S(1)}, f32[16,16,128]{2,1,0:T(8,128)S(1)}, u32[]{:S(2)}, u32[]{:S(2)}) %collective-permute-start) | collective-permute-done | bytes 131104 | tf_op jit(solution)/shard_map/ppermute | solution.py:342
  32.6 17.9 %all_to_all.11 = f32[16,16,128]{2,1,0:T(8,128)S(1)} all-to-all(f32[16,16,128]{2,1,0:T(8,128)S(1)} %add.12), channel_id=1, replica_groups=mesh['species'=8,'wave'=32] {'species'}, dimensions={0} | all-to-all | bytes 262144 | tf_op jit(solution)/shard_map/all_to_all | solution.py:343
  50.5 0.1 slice.24
  50.6 5.9 %all-gather = f32[4,16,64]{2,1,0:T(8,128)S(1)} all-gather(f32[2,16,64]{2,1,0:T(8,128)S(1)} %slice.24), channel_id=2, replica_groups={{1,2},{3,4},{5,6},{7,8},{9,10},{11,12},{13,14},{15,16},{17,18},{19,20},..., dimensions={0}, use_global_device_ids=true | all-gather | bytes 24576 | tf_op jit(solution)/shard_map/all_gather | solution.py:348
  56.5 0.1 copy.24
  56.6 0.7 %reshape.50 = f32[4,2,256]{2,1,0:T(2,128)} reshape(f32[4,2,16,16]{3,2,1,0:T(8,128)S(1)} %copy.25) | data formatting | bytes 16384 | tf_op jit(solution)/shard_map/reshape | solution.py:351
  (5 shorter events, 0.1 us)
Async XLA Ops:
  2.1 14.6 %copy-start = (f32[70,8,128]{2,1,0:T(8,128)S(1)}, f32[70,8,128]{2,1,0:T(8,128)}, u32[]{:S(2)}) copy-start(f32[70,8,128]{2,1,0:T(8,128)} %get-tuple-element.11.tables) | copy-start | bytes 860164
  31.1 1.4 %collective-permute-start = (f32[16,16,128]{2,1,0:T(8,128)S(1)}, f32[16,16,128]{2,1,0:T(8,128)S(1)}, u32[]{:S(2)}, u32[]{:S(2)}) collective-permute-start(f32[16,16,128]{2,1,0:T(8,128)S(1)} %get-tuple-element.13), channel_id=1, source_target_pairs={{0,1},{1,0},{2,3},{3,2},{4,5},{5,4},{6,7},{7,6},{8,9},{9,8},{10,11... | collective-permute-start | bytes 393224 | tf_op jit(solution)/shard_map/ppermute | solution.py:342
